TPU v7x, 256 devices: a whole 4x4x8 slice. The times are simulated.
256 devices in a mesh: section: 4 (over x), ep: 64 (over y, z, core).
Axes of the slice: x: 4, y: 4, z: 8, core: 2. Of those that a mesh axis runs over, the one named last changes fastest.
Arguments:
- hidden_in: bfloat16 [4, 64, 4096], P(None, 'ep'), may hold values from -4 to 4
- norm_gain: float32 [4, 4096], P('section'), may hold values from 0.1 to 1.9
- gate_weight: bfloat16 [4, 4096, 24576], P('section', None, 'ep'), may hold values from -0.09375 to 0.09375
- up_weight: bfloat16 [4, 4096, 24576], P('section', None, 'ep'), may hold values from -0.09375 to 0.09375
- down_weight: bfloat16 [4, 24576, 4096], P('section', 'ep'), may hold values from -0.15625 to 0.15625
- routes: int32 [4, 4, 64, 8], P('section'), may hold values from 0 to 15, all different within a row; in each aligned block of 64 rows (0 to 63, 64 to 127, ..., all dimensions but the last counted through in order) at most 48 rows name the same one
- route_weight: float32 [4, 4, 64, 8], P('section'), may hold values from 0.2 to 1
Outputs:
- hidden_out: bfloat16 [4, 4, 64, 4096], P('section', None, 'ep')
Inputs may be any that keep to these rules, and one draw needn't show every extreme that they name: `routes`: each row names 8 different experts; within one micro-batch of one layer at most 48 rows name one expert.
All inputs are finite; a program needn't handle non-finite values.
Results may differ from a plain program's by a relative error of at most 0.015.
Values may be sent and summed in bfloat16 or wider, within the bound.
A program may use at most 64 MiB of HBM per device.

v0:
```python
import jax
import jax.numpy as jnp
from jax import lax
from jax.sharding import PartitionSpec as P

FF_E = 1536


def passed_along(array, axis, by):
    length = lax.axis_size(axis)
    pairs = [(i, i + by) for i in range(length) if 0 <= i + by < length]
    return lax.ppermute(array, axis, pairs)


def expert_part(rows_in, w_gate, w_up, w_down):
    gate = jnp.dot(rows_in, w_gate, preferred_element_type=jnp.float32)
    upper = jnp.dot(rows_in, w_up, preferred_element_type=jnp.float32)
    act = (jax.nn.silu(gate) * upper).astype(jnp.bfloat16)
    return jnp.dot(act, w_down, preferred_element_type=jnp.float32)


def layer_step(current, gain, w_gate, w_up, w_down, named, weights, my_expert):
    current_f = current.astype(jnp.float32)
    square = jnp.mean(current_f * current_f, axis=-1, keepdims=True)
    normed = (current_f * lax.rsqrt(square + 1e-06) * gain).astype(jnp.bfloat16)
    whole = lax.all_gather(normed, "ep", axis=0, tiled=True)
    weights = weights / jnp.sum(weights, axis=-1, keepdims=True)
    coeff = jnp.sum(jnp.where(named == my_expert, weights, jnp.zeros_like(weights)), axis=-1)
    term = expert_part(whole, w_gate, w_up, w_down) * coeff[:, None]
    moe = lax.psum_scatter(term, "ep", scatter_dimension=0, tiled=True)
    return (current_f + moe).astype(jnp.bfloat16)


def local(hidden_in, norm_gain, gate_weight, up_weight, down_weight, routes, route_weight):
    sections = lax.axis_size("section")
    section = lax.axis_index("section")
    slices = FF_E // gate_weight.shape[2]
    my_expert = lax.axis_index("ep") // slices
    batches = hidden_in.shape[0]
    gain = norm_gain[0]
    results = jnp.zeros(hidden_in.shape, jnp.bfloat16)
    arriving = jnp.zeros(hidden_in.shape[1:], jnp.bfloat16)
    ticks = batches + sections - 1
    for tick in range(ticks):
        batch = tick - section
        valid = (batch >= 0) & (batch < batches)
        picked = jnp.clip(batch, 0, batches - 1)
        current = jnp.where(section == 0, hidden_in[min(tick, batches - 1)], arriving)
        named = lax.dynamic_index_in_dim(routes[0], picked, 0, keepdims=False)
        weights = lax.dynamic_index_in_dim(route_weight[0], picked, 0, keepdims=False)
        output = layer_step(
            current, gain, gate_weight[0], up_weight[0], down_weight[0], named, weights, my_expert
        )
        kept = lax.dynamic_index_in_dim(results, picked, 0, keepdims=False)
        results = lax.dynamic_update_index_in_dim(
            results, jnp.where(valid, output, kept), picked, 0
        )
        if tick + 1 < ticks:
            arriving = passed_along(output, "section", 1)
    return results[None]


def solution(mesh):
    return jax.shard_map(
        local,
        mesh=mesh,
        in_specs=(
            P(None, "ep", None),
            P("section", None),
            P("section", None, "ep"),
            P("section", None, "ep"),
            P("section", "ep", None),
            P("section", None, None, None),
            P("section", None, None, None),
        ),
        out_specs=P("section", None, "ep", None),
        check_vma=False,
    )
```

profile of v0, /device:TPU:7, one launch (start us, length us, event | category | flops | bytes accessed | tf_op | source)
XLA Modules:
  0.0 1762.0 jit_solution(2043356438850293305)
XLA Ops:
  6.6 1.6 multiply_reduce_fusion.6
  9.6 59.1 %all-gather = bf16[64,1,4096]{2,1,0:T(2,128)(2,1)} all-gather(bf16[1,1,4096]{2,1,0:T(2,128)(2,1)S(1)} %convert_bitcast_fusion.6), channel_id=1, replica_groups=mesh['section'=4,'ep'=64] {'ep'}, dimensions={0}, use_global_device_ids=true | all-gather | bytes 532480 | tf_op jit(solution)/shard_map/all_gather | solution.py:26
  68.7 3.1 fusion.33
  72.0 4.9 convolution_multiply_fusion.6
  77.6 180.2 %all-reduce.15.cloned.1.call-done = f32[64,4096]{1,0:T(8,128)} async-done(((f32[64,4096]{1,0:T(8,128)}), f32[64,4096]{1,0:T(8,128)}) %all-reduce.15.cloned.1.call-update) | async-done | bytes 1048592
  257.9 1.6 fusion.175
  259.4 1.3 collective-permute-start
  260.7 3.2 collective-permute-done
  265.3 52.2 %all-gather.1 = bf16[64,1,4096]{2,1,0:T(2,128)(2,1)S(1)} all-gather(bf16[1,1,4096]{2,1,0:T(2,128)(2,1)S(1)} %convert_bitcast_fusion.5), channel_id=1, replica_groups=mesh['section'=4,'ep'=64] {'ep'}, dimensions={0}, use_global_device_ids=true | all-gather | bytes 532480 | tf_op jit(solution)/shard_map/all_gather | solution.py:26
  318.5 2.8 fusion.31
  321.4 4.9 convolution_multiply_fusion.5
  326.6 180.2 %all-reduce.17.cloned.1.call-done = f32[64,4096]{1,0:T(8,128)} async-done(((f32[64,4096]{1,0:T(8,128)}), f32[64,4096]{1,0:T(8,128)}) %all-reduce.17.cloned.1.call-update) | async-done | bytes 1048592
  506.7 1.6 fusion.178
  508.3 1.3 collective-permute-start.1
  509.6 3.2 collective-permute-done.1
  514.1 52.7 %all-gather.2 = bf16[64,1,4096]{2,1,0:T(2,128)(2,1)S(1)} all-gather(bf16[1,1,4096]{2,1,0:T(2,128)(2,1)S(1)} %convert_bitcast_fusion.4), channel_id=1, replica_groups=mesh['section'=4,'ep'=64] {'ep'}, dimensions={0}, use_global_device_ids=true | all-gather | bytes 532480 | tf_op jit(solution)/shard_map/all_gather | solution.py:26
  567.8 2.8 fusion.29
  570.7 4.9 convolution_multiply_fusion.4
  575.8 180.2 %all-reduce.19.cloned.1.call-done = f32[64,4096]{1,0:T(8,128)} async-done(((f32[64,4096]{1,0:T(8,128)}), f32[64,4096]{1,0:T(8,128)}) %all-reduce.19.cloned.1.call-update) | async-done | bytes 1048592
  756.0 1.6 fusion.185
  757.6 1.3 collective-permute-start.2
  758.9 3.2 collective-permute-done.2
  763.4 52.2 %all-gather.3 = bf16[64,1,4096]{2,1,0:T(2,128)(2,1)S(1)} all-gather(bf16[1,1,4096]{2,1,0:T(2,128)(2,1)S(1)} %convert_bitcast_fusion.3), channel_id=1, replica_groups=mesh['section'=4,'ep'=64] {'ep'}, dimensions={0}, use_global_device_ids=true | all-gather | bytes 532480 | tf_op jit(solution)/shard_map/all_gather | solution.py:26
  816.7 2.8 fusion.27
  819.5 4.9 convolution_multiply_fusion.3
  824.7 180.2 %all-reduce.21.cloned.1.call-done = f32[64,4096]{1,0:T(8,128)} async-done(((f32[64,4096]{1,0:T(8,128)}), f32[64,4096]{1,0:T(8,128)}) %all-reduce.21.cloned.1.call-update) | async-done | bytes 1048592
  1004.9 1.6 fusion.186
  1006.4 1.3 collective-permute-start.3
  1007.7 3.2 collective-permute-done.3
  1012.3 52.4 %all-gather.4 = bf16[64,1,4096]{2,1,0:T(2,128)(2,1)S(1)} all-gather(bf16[1,1,4096]{2,1,0:T(2,128)(2,1)S(1)} %convert_bitcast_fusion.2), channel_id=1, replica_groups=mesh['section'=4,'ep'=64] {'ep'}, dimensions={0}, use_global_device_ids=true | all-gather | bytes 532480 | tf_op jit(solution)/shard_map/all_gather | solution.py:26
  1065.7 2.8 fusion.25
  1068.5 4.9 convolution_multiply_fusion.2
  1073.7 180.2 %all-reduce.23.cloned.1.call-done = f32[64,4096]{1,0:T(8,128)} async-done(((f32[64,4096]{1,0:T(8,128)}), f32[64,4096]{1,0:T(8,128)}) %all-reduce.23.cloned.1.call-update) | async-done | bytes 1048592
  1253.9 1.6 fusion.187
  1255.5 1.3 collective-permute-start.4
  1256.8 3.2 collective-permute-done.4
  1261.3 52.2 %all-gather.5 = bf16[64,1,4096]{2,1,0:T(2,128)(2,1)S(1)} all-gather(bf16[1,1,4096]{2,1,0:T(2,128)(2,1)S(1)} %convert_bitcast_fusion.1), channel_id=1, replica_groups=mesh['section'=4,'ep'=64] {'ep'}, dimensions={0}, use_global_device_ids=true | all-gather | bytes 532480 | tf_op jit(solution)/shard_map/all_gather | solution.py:26
  1314.6 2.8 fusion.23
  1317.4 4.9 convolution_multiply_fusion.1
  1322.6 180.2 %all-reduce.25.cloned.1.call-done = f32[64,4096]{1,0:T(8,128)} async-done(((f32[64,4096]{1,0:T(8,128)}), f32[64,4096]{1,0:T(8,128)}) %all-reduce.25.cloned.1.call-update) | async-done | bytes 1048592
  1502.7 1.6 fusion.188
  1505.6 3.2 collective-permute-done.5
  1510.1 52.4 %all-gather.6 = bf16[64,1,4096]{2,1,0:T(2,128)(2,1)S(1)} all-gather(bf16[1,1,4096]{2,1,0:T(2,128)(2,1)S(1)} %convert_bitcast_fusion), channel_id=1, replica_groups=mesh['section'=4,'ep'=64] {'ep'}, dimensions={0}, use_global_device_ids=true | all-gather | bytes 532480 | tf_op jit(solution)/shard_map/all_gather | solution.py:26
  1563.6 2.8 fusion.21
  1566.4 5.0 convolution_multiply_fusion
  1571.6 180.3 %all-reduce.27.cloned.1.call-done = f32[64,4096]{1,0:T(8,128)} async-done(((f32[64,4096]{1,0:T(8,128)}), f32[64,4096]{1,0:T(8,128)}) %all-reduce.27.cloned.1.call-update) | async-done | bytes 1048592
  1751.9 1.6 fusion.189
  1753.5 1.4 dynamic_update_slice.29
  (64 shorter events, 14.2 us)
Async XLA Ops:
  6.5 65.4 %copy-start = (bf16[1,384,4096]{2,1,0:T(8,128)(2,1)S(1)}, bf16[1,384,4096]{2,1,0:T(8,128)(2,1)}, u32[]{:S(2)}) copy-start(bf16[1,384,4096]{2,1,0:T(8,128)(2,1)} %param.11) | copy-start | bytes 9437188
  6.5 65.3 %copy-start.10 = (f32[1,4,64,8]{2,3,1,0:T(8,128)S(1)}, f32[1,4,64,8]{2,3,1,0:T(8,128)}, u32[]{:S(2)}) copy-start(f32[1,4,64,8]{2,3,1,0:T(8,128)} %param.13) | copy-start | bytes 24580
  6.5 65.4 %copy-start.11 = (s32[1,4,64,8]{2,3,1,0:T(8,128)S(1)}, s32[1,4,64,8]{2,3,1,0:T(8,128)}, u32[]{:S(2)}) copy-start(s32[1,4,64,8]{2,3,1,0:T(8,128)} %param.12) | copy-start | bytes 24580
  6.5 251.3 %all-reduce.15.cloned.1.call-start = ((), (), s32[]{:S(2)}) async-start(), calls=%async_computation | async-start | bytes 2097152
  72.0 5.1 copy-start.12
  72.0 185.9 %copy-start.8 = (bf16[4,1,4096]{2,0,1:T(4,128)(2,1)S(1)}, bf16[4,1,4096]{2,0,1:T(4,128)(2,1)}, u32[]{:S(2)}) copy-start(bf16[4,1,4096]{2,0,1:T(4,128)(2,1)} %param.7) | copy-start | bytes 98308
  72.0 193.3 %copy-start.7 = (f32[1,4096]{1,0:T(1,128)S(1)}, f32[1,4096]{1,0:T(1,128)}, u32[]{:S(2)}) copy-start(f32[1,4096]{1,0:T(1,128)} %param.8) | copy-start | bytes 49156
  77.0 429.8 %all-reduce.17.cloned.1.call-start = ((), (), s32[]{:S(2)}) async-start(), calls=%async_computation.1 | async-start | bytes 2097152
  259.4 4.5 collective-permute-start
  317.5 1.0 copy-start.2
  326.3 429.7 %all-reduce.19.cloned.1.call-start = ((), (), s32[]{:S(2)}) async-start(), calls=%async_computation.2 | async-start | bytes 2097152
  508.3 4.5 collective-permute-start.1
  566.8 1.0 copy-start.3
  575.6 429.2 %all-reduce.21.cloned.1.call-start = ((), (), s32[]{:S(2)}) async-start(), calls=%async_computation.3 | async-start | bytes 2097152
  757.6 4.5 collective-permute-start.2
  815.6 1.0 copy-start.4
  824.5 429.4 %all-reduce.23.cloned.1.call-start = ((), (), s32[]{:S(2)}) async-start(), calls=%async_computation.4 | async-start | bytes 2097152
  1006.4 4.5 collective-permute-start.3
  1064.7 1.0 copy-start.5
  1073.5 429.3 %all-reduce.25.cloned.1.call-start = ((), (), s32[]{:S(2)}) async-start(), calls=%async_computation.5 | async-start | bytes 2097152
  1255.5 4.5 collective-permute-start.4
  1313.5 1.0 copy-start.6
  1322.3 429.6 %all-reduce.27.cloned.1.call-start = ((), (), s32[]{:S(2)}) async-start(), calls=%async_computation.6 | async-start | bytes 2097152
  1504.3 4.5 collective-permute-start.5
  1562.6 1.0 copy-start.1
  1571.6 181.9 %copy-start.9 = (bf16[4,1,4096]{2,0,1:T(4,128)(2,1)}, bf16[4,1,4096]{2,0,1:T(4,128)(2,1)S(1)}, u32[]{:S(2)}) copy-start(bf16[4,1,4096]{2,0,1:T(4,128)(2,1)S(1)} %dynamic_update_slice.28) | copy-start | bytes 98308
Sparse Core Ops, SparseCore 0:
  77.1 180.7 all-reduce.14
  326.4 180.2 all-reduce.16
  575.7 180.2 all-reduce.18
  824.6 180.2 all-reduce.20
  1073.6 180.2 all-reduce.22
  1322.4 180.2 all-reduce.24
  1571.5 180.3 all-reduce.26
where the time goes:
time: 1770 us; the launch traced here: 1760 us
  waiting for transfers between devices  1280 us (72%)
  blocking collectives  373 us (21%)
  matrix products  54.6 us (3%)
  between operations  18.9 us (1%)
    unnamed x14, waiting for transfers between devices  1260 us
    all_gather x7, blocking collectives, layer_step(): whole = lax.all_gather(normed, 'ep', axis=0, tiled=True)  373 us
  transfers between devices with their start and end apart: 13, of which 13 were waited for; matrix products, arithmetic and copies ran while one was open for 0% of the time, Pallas kernels for 0%

commit v1 on v0

v1 whole, which is shorter than its diff:
```python
import functools

import jax
import jax.numpy as jnp
from jax import lax
from jax.experimental import pallas as pl
from jax.experimental.pallas import tpu as pltpu
from jax.sharding import PartitionSpec as P

MESH = pl.DeviceIdType.MESH
BF = jnp.bfloat16
F32 = jnp.float32

D = 4096
FF = 384
MB = 4
SECTIONS = 4
YS, ZS = 4, 8
ROWS = 64
RB = 16
FB = 256
HALF = D // 2
CH = 512
FAR_FIRST = (4, 3, 5, 2, 6, 1, 7)
NEAR_FIRST = (0, 1, 7, 2, 6, 3, 5, 4)
CHUNK_ORDER = (2, 1, 3, 0)

SCHEDULE = (("A", 0), ("E", 2), ("C", 1), ("D", 1), ("F", 2), ("B", 0))
SLOTS = MB + 2


def mo(value, by):
    return pl.multiple_of(value, by)


def wait(ref, sem):
    pltpu.make_async_copy(ref, ref, sem).wait()


def kernel(
    hin, gain, wg_hbm, wu_hbm, wd_hbm, routes, rweight, out,
    wg, wu, wd, xg, hin_f, tin, coeff, act_s, pc, rsc, part, py, rsy, pz, rsz,
    res, oblk, out_t, orow,
    w_sem, tin_r, tin_s, agz_r, agy_r, agc_r, rsc_r, rsy_r, rsz_r, res_r, ob_r, or_r, or_s,
    s_a, s_res, s_ob, s_b, s_c, s_d, s_e, s_f,
):
    s = lax.axis_index("section")
    ep = lax.axis_index("ep")
    y = ep // 16
    q = ep % 16
    z = q // 2
    c = q % 2
    b = c * ZS + z
    plane = y * 16
    partner = (s, plane + z * 2 + (1 - c))
    row0 = mo(y * RB, RB)
    col0 = mo(b * FB, FB)
    half0 = mo(c * HALF, HALF)
    half1 = mo((1 - c) * HALF, HALF)

    def at(sec, yy, zz, cc):
        return (sec, yy * 16 + zz * 2 + cc)

    def send(src, dst, ss, rs, device):
        pltpu.make_async_remote_copy(
            src_ref=src, dst_ref=dst, send_sem=ss, recv_sem=rs, device_id=device, device_id_type=MESH
        ).start()

    weights = [
        pltpu.make_async_copy(wg_hbm.at[0], wg, w_sem.at[0]),
        pltpu.make_async_copy(wu_hbm.at[0], wu, w_sem.at[1]),
        pltpu.make_async_copy(wd_hbm.at[0], wd, w_sem.at[2]),
    ]
    for copy in weights:
        copy.start()

    barrier = pltpu.get_barrier_semaphore()

    def greet(device):
        pl.semaphore_signal(barrier, inc=1, device_id=device, device_id_type=MESH)

    def greet_plane(j, _):
        greet((s, plane + (q + j) % 16))
        return 0

    lax.fori_loop(1, 16, greet_plane, 0)
    for dy in (1, 2, 3):
        greet(at(s, (y + dy) % YS, z, c))

    def greet_next(j, _):
        greet(at(s + 1, y, j, c))
        return 0

    def greet_last(j, _):
        greet(at(s - 1, y, j, c))
        return 0

    @pl.when(s < SECTIONS - 1)
    def _():
        lax.fori_loop(0, ZS, greet_next, 0)

    @pl.when(s > 0)
    def _():
        lax.fori_loop(0, ZS, greet_last, 0)

    expert = ep // 4
    rw = rweight[0].reshape(MB * ROWS, 8)
    named = routes[0].reshape(MB * ROWS, 8) == expert
    hit = jnp.sum(jnp.where(named, rw, 0.0), axis=-1, keepdims=True)
    total = jnp.sum(rw, axis=-1, keepdims=True)
    coeff[...] = jnp.broadcast_to(hit / total, (MB * ROWS, 128))
    hin_f[...] = jnp.zeros_like(hin_f)
    hin_f[0:MB, :] = hin[:, 0, :].astype(F32)
    out_t[...] = jnp.zeros_like(out_t)

    inner = jnp.logical_and(s > 0, s < SECTIONS - 1)
    pl.semaphore_wait(barrier, jnp.where(inner, 18 + 2 * ZS, 18 + ZS))

    @pl.when(s == 0)
    def _():
        def spread(j, _):
            qq = (q + j) % 16
            bb = (qq % 2) * ZS + qq // 2
            send(hin_f.at[:, pl.ds(mo(bb * FB, FB), FB)], tin.at[q], tin_s, tin_r, (s, plane + qq))
            return 0

        lax.fori_loop(1, 16, spread, 0)
        tin[q] = hin_f[:, pl.ds(col0, FB)]
        wait(tin.at[pl.ds(0, 15)], tin_r)

    def block(m, yy, bb):
        return xg.at[m, pl.ds(mo(yy * RB, RB), RB), pl.ds(mo(bb * FB, FB), FB)]

    def summed(where, m, start):
        total = start
        for k in range(ZS):
            total = total + rsz[where, m, k].astype(F32)
        return total

    def phase_a(m):
        @pl.when(s == 0)
        def _():
            xg[m, pl.ds(row0, RB), pl.ds(col0, FB)] = tin[:, m, :].astype(BF)

        @pl.when(s > 0)
        def _():
            wait(res.at[m], res_r.at[m])
            wait(rsz.at[0, m], rsz_r.at[0, m])
            xg[m, pl.ds(row0, RB), pl.ds(col0, FB)] = summed(0, m, res[m].astype(F32)).astype(BF)

        mine = block(m, y, b)
        for off in FAR_FIRST:
            send(mine, mine, s_a.at[m], agz_r.at[m, z], at(s, y, (z + off) % ZS, c))

        @pl.when(s < SECTIONS - 1)
        def _():
            send(mine, res.at[m], s_res.at[m], res_r.at[m], at(s + 1, y, z, c))

        @pl.when(s > 0)
        def _():
            send(mine, oblk.at[m], s_ob.at[m], ob_r.at[m], at(s - 1, y, z, c))

    def phase_b(m):
        for off in NEAR_FIRST:
            zz = (z + off) % ZS
            piece = block(m, y, c * ZS + zz)
            if off:
                wait(piece, agz_r.at[m, zz])
            for dy in (2, 1, 3):
                send(piece, piece, s_b.at[m], agy_r.at[m, dy - 1], at(s, (y + dy) % YS, z, c))
        rows = xg.at[m, pl.ds(row0, RB), pl.ds(half0, HALF)]
        send(rows, rows, s_c.at[m], agc_r.at[m], partner)

    def phase_c(m):
        for dy in (1, 3, 2):
            yy = (y + YS - dy) % YS
            rows = xg.at[m, pl.ds(mo(yy * RB, RB), RB), pl.ds(half0, HALF)]
            wait(rows, agy_r.at[m, dy - 1])
            send(rows, rows, s_c.at[m], agc_r.at[m], partner)

    def phase_d(m):
        def up_to(start, carry):
            g, u, ss = carry
            for k in range(HALF // CH):
                cols = pl.ds(mo(start + k * CH, CH), CH)
                h = xg[m, :, cols].astype(F32)
                sq = h * h
                for j in range(CH // 128):
                    ss = ss + sq[:, j * 128 : (j + 1) * 128]
                hg = (h * gain[:, cols]).astype(BF)
                g = g + jnp.dot(hg, wg[cols, :], preferred_element_type=F32)
                u = u + jnp.dot(hg, wu[cols, :], preferred_element_type=F32)
            return g, u, ss

        carry = (jnp.zeros((ROWS, FF), F32), jnp.zeros((ROWS, FF), F32), jnp.zeros((ROWS, 128), F32))
        carry = up_to(half0, carry)
        wait(xg.at[m, :, pl.ds(half1, HALF)], agc_r.at[m])
        g, u, ss = up_to(half1, carry)
        scale = lax.rsqrt(jnp.sum(ss, axis=-1, keepdims=True) * (1.0 / D) + 1e-06)
        g = g * scale
        co = coeff[pl.ds(mo(m * ROWS, ROWS), ROWS), 0:1]
        act_s[...] = (jax.nn.silu(g) * (u * scale) * co).astype(BF)
        for t, off in enumerate(CHUNK_ORDER):
            piece = (z // 2 + off) % 4
            src = mo((1 - c) * HALF + piece * CH, CH)
            cols = pl.ds(mo(piece * CH, CH), CH)
            pc[m, :, cols] = jnp.dot(act_s[...], wd[:, pl.ds(src, CH)], preferred_element_type=F32).astype(BF)
            send(pc.at[m, :, cols], rsc.at[m, :, cols], s_d.at[m], rsc_r.at[m, t], partner)
        for off in CHUNK_ORDER:
            piece = (z // 2 + off) % 4
            src = mo(c * HALF + piece * CH, CH)
            cols = pl.ds(mo(piece * CH, CH), CH)
            part[m, :, cols] = jnp.dot(act_s[...], wd[:, pl.ds(src, CH)], preferred_element_type=F32)

    def phase_e(m):
        for t, off in enumerate(CHUNK_ORDER):
            cols = pl.ds(mo(((z // 2 + off) % 4) * CH, CH), CH)
            wait(rsc.at[m, :, cols], rsc_r.at[m, t])
            py[m, :, cols] = (part[m, :, cols] + rsc[m, :, cols].astype(F32)).astype(BF)
            for dy in (2, 1, 3):
                yy = (y + dy) % YS
                send(
                    py.at[m, pl.ds(mo(yy * RB, RB), RB), cols],
                    rsy.at[m, pl.ds((dy - 1) * RB, RB), cols],
                    s_e.at[m], rsy_r.at[m, t], at(s, yy, z, c),
                )

    def phase_f(m):
        last = s == SECTIONS - 1
        to = jnp.where(last, s, s + 1)
        where = jnp.where(last, 1, 0)
        for t, off in enumerate(CHUNK_ORDER):
            piece = (z // 2 + off) % 4
            cols = pl.ds(mo(piece * CH, CH), CH)
            wait(rsy.at[m, :, cols], rsy_r.at[m, t])
            total = py[m, pl.ds(row0, RB), cols].astype(F32)
            for k in range(YS - 1):
                total = total + rsy[m, k * RB : (k + 1) * RB, cols].astype(F32)
            pz[m, :, cols] = total.astype(BF)
            for e in range(2):
                zz = piece * 2 + e
                src = pz.at[m, :, pl.ds(mo(zz * FB, FB), FB)]
                dst = rsz.at[where, m, z]
                here = jnp.logical_and(last, zz == z)

                @pl.when(here)
                def _():
                    pltpu.make_async_copy(src, dst, rsz_r.at[where, m]).start()

                @pl.when(jnp.logical_not(here))
                def _():
                    send(src, dst, s_f.at[m], rsz_r.at[where, m], at(to, y, zz, c))

    phases = {"A": phase_a, "B": phase_b, "C": phase_c, "D": phase_d, "E": phase_e, "F": phase_f}

    def slot(n, _):
        for name, lag in SCHEDULE:
            m = n - lag

            if name == "D":
                @pl.when(m == 0)
                def _():
                    for copy in weights:
                        copy.wait()

            @pl.when(jnp.logical_and(m >= 0, m < MB))
            def _():
                phases[name](m)

        return 0

    lax.fori_loop(0, SLOTS, slot, 0)

    for m in range(MB):
        @pl.when(s == SECTIONS - 1)
        def _():
            wait(rsz.at[1, m], rsz_r.at[1, m])
            start = xg[m, pl.ds(row0, RB), pl.ds(col0, FB)].astype(F32)
            oblk[m] = summed(1, m, start).astype(BF)

        @pl.when(s < SECTIONS - 1)
        def _():
            wait(oblk.at[m], ob_r.at[m])

        out_t[:, m, :] = oblk[m].astype(F32)

    def collect(j, _):
        qq = (q + j) % 16
        send(out_t.at[qq], orow.at[b], or_s, or_r, (s, plane + qq))
        return 0

    lax.fori_loop(1, 16, collect, 0)
    orow[b] = out_t[q]
    wait(orow.at[pl.ds(0, 15)], or_r)
    for k in range(2 * ZS):
        out[0, :, 0, k * FB : (k + 1) * FB] = orow[k, 0:MB, :].astype(BF)

    @pl.when(s == 0)
    def _():
        wait(tin.at[pl.ds(0, 15)], tin_s)

    wait(orow.at[pl.ds(0, 15)], or_s)
    for m in range(MB):
        wait(xg.at[m, pl.ds(0, RB), pl.ds(0, 7 * FB)], s_a.at[m])
        wait(xg.at[m, pl.ds(0, 3 * RB), pl.ds(0, HALF)], s_b.at[m])
        wait(xg.at[m, :, pl.ds(0, HALF)], s_c.at[m])
        wait(pc.at[m], s_d.at[m])
        wait(rsy.at[m], s_e.at[m])

        @pl.when(s < SECTIONS - 1)
        def _():
            wait(rsz.at[0, m], s_f.at[m])
            wait(res.at[m], s_res.at[m])

        @pl.when(s == SECTIONS - 1)
        def _():
            wait(rsz.at[0, m, pl.ds(0, ZS - 1)], s_f.at[m])

        @pl.when(s > 0)
        def _():
            wait(oblk.at[m], s_ob.at[m])


def local(hidden_in, norm_gain, gate_weight, up_weight, down_weight, routes, route_weight):
    vmem = pl.BlockSpec(memory_space=pltpu.VMEM)
    hbm = pl.BlockSpec(memory_space=pl.ANY)
    dma = pltpu.SemaphoreType.DMA
    return pl.pallas_call(
        kernel,
        name="moe_layers",
        out_shape=jax.ShapeDtypeStruct((1, MB, 1, D), BF),
        in_specs=[vmem, vmem, hbm, hbm, hbm, vmem, vmem],
        out_specs=vmem,
        scratch_shapes=[
            pltpu.VMEM((D, FF), BF),
            pltpu.VMEM((D, FF), BF),
            pltpu.VMEM((FF, D), BF),
            pltpu.VMEM((MB, ROWS, D), BF),
            pltpu.VMEM((8, D), F32),
            pltpu.VMEM((16, 8, FB), F32),
            pltpu.VMEM((MB * ROWS, 128), F32),
            pltpu.VMEM((ROWS, FF), BF),
            pltpu.VMEM((MB, ROWS, HALF), BF),
            pltpu.VMEM((MB, ROWS, HALF), BF),
            pltpu.VMEM((MB, ROWS, HALF), F32),
            pltpu.VMEM((MB, ROWS, HALF), BF),
            pltpu.VMEM((MB, 3 * RB, HALF), BF),
            pltpu.VMEM((MB, RB, HALF), BF),
            pltpu.VMEM((2, MB, ZS, RB, FB), BF),
            pltpu.VMEM((MB, RB, FB), BF),
            pltpu.VMEM((MB, RB, FB), BF),
            pltpu.VMEM((16, 8, FB), F32),
            pltpu.VMEM((16, 8, FB), F32),
            dma((3,)),
            dma, dma,
            dma((MB, ZS)),
            dma((MB, 3)),
            dma((MB,)),
            dma((MB, 4)),
            dma((MB, 4)),
            dma((2, MB)),
            dma((MB,)),
            dma((MB,)),
            dma, dma,
            dma((MB,)), dma((MB,)), dma((MB,)), dma((MB,)), dma((MB,)), dma((MB,)), dma((MB,)), dma((MB,)),
        ],
        compiler_params=pltpu.CompilerParams(
            collective_id=0, has_side_effects=True, vmem_limit_bytes=48 << 20
        ),
        cost_estimate=pl.CostEstimate(
            flops=6 * MB * ROWS * D * FF, bytes_accessed=6 * D * FF, transcendentals=MB * ROWS * FF
        ),
    )(hidden_in, norm_gain, gate_weight, up_weight, down_weight, routes, route_weight)


def solution(mesh):
    return jax.shard_map(
        local,
        mesh=mesh,
        in_specs=(
            P(None, "ep", None),
            P("section", None),
            P("section", None, "ep"),
            P("section", None, "ep"),
            P("section", "ep", None),
            P("section", None, None, None),
            P("section", None, None, None),
        ),
        out_specs=P("section", None, "ep", None),
        check_vma=False,
    )
```

time: 1770 us -> 157 us (0.09)
  waiting for transfers between devices: 1280 us -> 0 us
  blocking collectives: 373 us -> 0 us
  Pallas kernels: 0 us -> 151 us
  matrix products: 54.6 us -> 0 us
  between operations: 18.9 us -> 0.04 us
    unnamed x14 -> x0, waiting for transfers between devices: 1260 us -> none
    all_gather x7 -> x0, blocking collectives: 373 us -> none  [layer_step(): whole = lax.all_gather(normed, 'ep', axis=0, tiled=True)]
    pallas_call x0 -> x1, Pallas kernels: none -> 151 us  [local(): pl.pallas_call(kernel, name='moe_layers', out_shape=jax.ShapeDtypeStruct(...]
    dot_general x14 -> x0, matrix products: 54.6 us -> none  [the longest x7 34.6 us: expert_part(): return jnp.dot(act, w_down, preferred_element_type=jnp.float32)]
    ppermute x6 -> x0, waiting for transfers between devices: 19.1 us -> none  [passed_along(): return lax.ppermute(array, axis, pairs)]
  transfers between devices with their start and end apart: 13 -> 0, of which waited for: 13 -> 0; matrix products, arithmetic and copies ran while one was open for 0% -> 0% of each run, Pallas kernels for 0% -> 0%
where the time goes in v1:
time: 157 us
  Pallas kernels  151 us (96%)
  local copies, waits for them, and re-layouts  5.69 us (4%)
    pallas_call x1, Pallas kernels, local(): pl.pallas_call(kernel, name='moe_layers', out_shape=jax.ShapeDtypeStruct(...  151 us
    unnamed x7, local copies, waits for them, and re-layouts  5.03 us

profile of v1, /device:TPU:7, one launch (start us, length us, event | category | flops | bytes accessed | tf_op | source)
XLA Modules:
  0.0 156.5 jit_solution(12764590439393312179)
XLA Ops:
  0.0 0.8 copy.8.hin
  0.8 0.8 copy.9.routes
  1.6 0.8 copy.10.rweight
  2.4 0.0 copy-start
  2.5 1.9 %copy-done = bf16[1,4096,384]{2,1,0:T(8,128)(2,1)S(1)} copy-done((bf16[1,4096,384]{2,1,0:T(8,128)(2,1)S(1)}, bf16[1,4096,384]{2,1,0:T(8,128)(2,1)}, u32[]{:S(2)}) %copy-start) | copy-done | bytes 3145752
  4.3 0.0 copy-start.1
  4.3 0.7 copy-done.1
  5.1 150.8 %moe_layers.1 = bf16[1,4,1,4096]{3,2,1,0:T(2,128)(2,1)S(1)} custom-call(bf16[4,1,4096]{2,1,0:T(2,128)(2,1)S(1)} %copy.8.hin, f32[1,4096]{1,0:T(1,128)S(1)} %copy-done.1, bf16[1,4096,384]{2,1,0:T(8,128)(2,1)S(1)} %copy-done, bf16[1,4096,384]{2,1,0:T(8,128)(2,1)} %wu_hbm.1, bf16[1,384,4096]{2,1,0:T(8,128)(2,1)} %wd_hbm.1, s32[1,4,64,8]{3,2,1,0:T(8,128)S(1)} %copy.9.routes, ...), custom_call_target="tpu_custom_call" | custom-call | flops 2415919104 | bytes 9437184 | tf_op jit(solution)/shard_map/moe_layers/pallas_call | solution.py:328
  155.9 0.7 copy.11
Async XLA Ops:
  2.4 1.9 %copy-start = (bf16[1,4096,384]{2,1,0:T(8,128)(2,1)S(1)}, bf16[1,4096,384]{2,1,0:T(8,128)(2,1)}, u32[]{:S(2)}) copy-start(bf16[1,4096,384]{2,1,0:T(8,128)(2,1)} %wg_hbm.1) | copy-start | bytes 9437188
  4.3 0.7 copy-start.1

commit v2 on v1

v2 whole, which is shorter than its diff:
```python
import functools

import jax
import jax.numpy as jnp
from jax import lax
from jax.experimental import pallas as pl
from jax.experimental.pallas import tpu as pltpu
from jax.sharding import PartitionSpec as P

MESH = pl.DeviceIdType.MESH
BF = jnp.bfloat16
F32 = jnp.float32

D = 4096
FF = 384
MB = 4
SECTIONS = 4
YS, ZS = 4, 8
ROWS = 64
RB = 16
FB = 256
HALF = D // 2
CH = 512
PIECES = HALF // CH
FAR_FIRST = (4, 3, 5, 2, 6, 1, 7)
GATHER_ORDER = (0, 1, 3, 2)
SUM_ORDER = (2, 1, 3, 0)

SCHEDULE = (("A", 0), ("D", 2), ("G", 2), ("F", 3), ("E", 2), ("C", 1), ("B", 0))
SLOTS = MB + 3


def mo(value, by):
    return pl.multiple_of(value, by)


def wait(ref, sem):
    pltpu.make_async_copy(ref, ref, sem).wait()


def kernel(
    hin_hbm, gain_hbm, wg_hbm, wu_hbm, wd_hbm, routes_hbm, rweight_hbm, out,
    hin, gain, routes, rweight, wg, wu, wd, xg, hin_f, tin, coeff, act_s, pc, rsc, part, py, rsy, pz, rsz,
    res, oblk, out_t, orow, hin_0, tin_0, pzf, orow_l,
    w_sem, tin_r, tin_s, tin0_r, tin0_s, orl_r, agz_r, agy_r, agc_r, rsc_r, rsy_r, rsz_r, res_r, ob_r, or_r, or_s,
    s_a, s_res, s_ob, s_b, s_c, s_d, s_e, s_f,
):
    s = lax.axis_index("section")
    ep = lax.axis_index("ep")
    y = ep // 16
    q = ep % 16
    z = q // 2
    c = q % 2
    b = c * ZS + z
    plane = y * 16
    partner = (s, plane + z * 2 + (1 - c))
    row0 = mo(y * RB, RB)
    col0 = mo(b * FB, FB)
    half0 = mo(c * HALF, HALF)
    half1 = mo((1 - c) * HALF, HALF)

    def at(sec, yy, zz, cc):
        return (sec, yy * 16 + zz * 2 + cc)

    def send(src, dst, ss, rs, device):
        pltpu.make_async_remote_copy(
            src_ref=src, dst_ref=dst, send_sem=ss, recv_sem=rs, device_id=device, device_id_type=MESH
        ).start()

    small = [
        pltpu.make_async_copy(hin_hbm, hin, w_sem.at[3]),
        pltpu.make_async_copy(gain_hbm, gain, w_sem.at[4]),
        pltpu.make_async_copy(routes_hbm, routes, w_sem.at[5]),
        pltpu.make_async_copy(rweight_hbm, rweight, w_sem.at[6]),
    ]
    for copy in small:
        copy.start()
    weights = [
        pltpu.make_async_copy(wg_hbm.at[0], wg, w_sem.at[0]),
        pltpu.make_async_copy(wu_hbm.at[0], wu, w_sem.at[1]),
        pltpu.make_async_copy(wd_hbm.at[0], wd, w_sem.at[2]),
    ]
    for copy in weights:
        copy.start()

    barrier = pltpu.get_barrier_semaphore()

    def greet(device):
        pl.semaphore_signal(barrier, inc=1, device_id=device, device_id_type=MESH)

    def greet_plane(j, _):
        greet((s, plane + (q + j) % 16))
        return 0

    lax.fori_loop(1, 16, greet_plane, 0)
    for dy in (1, 2, 3):
        greet(at(s, (y + dy) % YS, z, c))

    def greet_next(j, _):
        greet(at(s + 1, y, j, c))
        return 0

    def greet_last(j, _):
        greet(at(s - 1, y, j, c))
        return 0

    @pl.when(s < SECTIONS - 1)
    def _():
        lax.fori_loop(0, ZS, greet_next, 0)

    @pl.when(s > 0)
    def _():
        lax.fori_loop(0, ZS, greet_last, 0)

    for copy in small:
        copy.wait()
    expert = ep // 4
    for m in range(MB):
        rw = rweight[0, m]
        hit = jnp.sum(jnp.where(routes[0, m] == expert, rw, 0.0), axis=0, keepdims=True)
        share = hit / jnp.sum(rw, axis=0, keepdims=True)
        coeff[m] = jnp.swapaxes(jnp.broadcast_to(share, (128, ROWS)), 0, 1)
    hin_f[...] = jnp.zeros_like(hin_f)
    hin_f[0:MB, :] = hin[...].astype(F32)
    for k in range(2 * ZS):
        hin_0[k // ZS, k % ZS : k % ZS + 1, :] = hin_f[0:1, k * FB : (k + 1) * FB]
    out_t[...] = jnp.zeros_like(out_t)

    inner = jnp.logical_and(s > 0, s < SECTIONS - 1)
    pl.semaphore_wait(barrier, jnp.where(inner, 18 + 2 * ZS, 18 + ZS))

    def ring(k):
        return (q + 8 + (1 - 2 * (k % 2)) * ((k + 1) // 2)) % 16

    @pl.when(s == 0)
    def _():
        def spread_0(k, _):
            qq = ring(k)
            send(hin_0.at[qq % 2], tin_0.at[q], tin0_s, tin0_r, (s, plane + qq))
            return 0

        lax.fori_loop(0, 15, spread_0, 0)
        pltpu.make_async_copy(hin_0.at[c], tin_0.at[q], tin0_r).start()

    def block(m, yy, bb):
        return xg.at[m, pl.ds(mo(yy * RB, RB), RB), pl.ds(mo(bb * FB, FB), FB)]

    def phase_a(m):
        first = jnp.logical_and(s == 0, m == 0)

        @pl.when(first)
        def _():
            wait(tin_0, tin0_r)
            for k in range(ZS):
                xg[m, pl.ds(row0, RB), pl.ds(mo(half0 + k * FB, FB), FB)] = tin_0[:, k, :].astype(BF)

            def spread(k, _):
                qq = ring(k)
                bb = (qq % 2) * ZS + qq // 2
                send(hin_f.at[:, pl.ds(mo(bb * FB, FB), FB)], tin.at[q], tin_s, tin_r, (s, plane + qq))
                return 0

            lax.fori_loop(0, 15, spread, 0)
            tin[q] = hin_f[:, pl.ds(col0, FB)]

        @pl.when(jnp.logical_and(s == 0, m == 1))
        def _():
            wait(tin.at[pl.ds(0, 15)], tin_r)

        @pl.when(jnp.logical_and(s == 0, m > 0))
        def _():
            xg[m, pl.ds(row0, RB), pl.ds(col0, FB)] = tin[:, m, :].astype(BF)

        @pl.when(s > 0)
        def _():
            wait(res.at[m], res_r.at[m])
            wait(rsz.at[m], rsz_r.at[m])
            total = res[m].astype(F32)
            for k in range(ZS):
                total = total + rsz[m, k].astype(F32)
            xg[m, pl.ds(row0, RB), pl.ds(col0, FB)] = total.astype(BF)

        mine = block(m, y, b)

        @pl.when(jnp.logical_not(first))
        def _():
            for off in FAR_FIRST:
                send(mine, mine, s_a.at[m], agz_r.at[m, z], at(s, y, (z + off) % ZS, c))

        @pl.when(s < SECTIONS - 1)
        def _():
            send(mine, res.at[m], s_res.at[m], res_r.at[m], at(s + 1, y, z, c))

        @pl.when(s > 0)
        def _():
            send(mine, oblk.at[m], s_ob.at[m], ob_r.at[m], at(s - 1, y, z, c))

    def gather_cols(t, start):
        return pl.ds(mo(start + ((z // 2 + GATHER_ORDER[t]) % PIECES) * CH, CH), CH)

    def phase_b(m):
        for t in range(PIECES):
            @pl.when(jnp.logical_or(s > 0, m > 0))
            def _():
                pair = ((z // 2 + GATHER_ORDER[t]) % PIECES) * 2
                for zz in (pair + 1 - z % 2,) if t == 0 else (pair, pair + 1):
                    wait(block(m, y, c * ZS + zz), agz_r.at[m, zz])

            piece = xg.at[m, pl.ds(row0, RB), gather_cols(t, half0)]
            for dy in (2, 1, 3):
                send(piece, piece, s_b.at[m], agy_r.at[m, t], at(s, (y + dy) % YS, z, c))

    def to_partner(m, t):
        cols = gather_cols(t, half0)
        wait(xg.at[m, pl.ds(0, 3 * RB), cols], agy_r.at[m, t])
        piece = xg.at[m, :, cols]
        send(piece, piece, s_c.at[m], agc_r.at[m, t], partner)

    def products(m, cols, carry):
        g, u, ss = carry
        h = xg[m, :, cols].astype(F32)
        sq = h * h
        for j in range(CH // 128):
            ss = ss + sq[:, j * 128 : (j + 1) * 128]
        hg = (h * gain[:, cols]).astype(BF)
        g = g + jnp.dot(hg, wg[cols, :], preferred_element_type=F32)
        u = u + jnp.dot(hg, wu[cols, :], preferred_element_type=F32)
        return g, u, ss

    def from_partner(m, t, carry):
        cols = gather_cols(t, half1)
        wait(xg.at[m, :, cols], agc_r.at[m, t])
        return products(m, cols, carry)

    def start_sums():
        return jnp.zeros((ROWS, FF), F32), jnp.zeros((ROWS, FF), F32), jnp.zeros((ROWS, 128), F32)

    def activate(m, carry):
        g, u, ss = carry
        scale = lax.rsqrt(jnp.sum(ss, axis=-1, keepdims=True) * (1.0 / D) + 1e-06)
        g = g * scale
        act_s[m] = (jax.nn.silu(g) * (u * scale) * coeff[m, :, 0:1]).astype(BF)

    def phase_c(m):
        for t in range(PIECES):
            to_partner(m, t)

    def phase_d(m):
        carry = start_sums()
        for t in range(PIECES):
            carry = products(m, gather_cols(t, half0), carry)
        for t in range(PIECES):
            carry = from_partner(m, t, carry)
        activate(m, carry)

    def phase_k(m):
        carry = start_sums()
        for t in range(PIECES):
            to_partner(m, t)
            carry = products(m, gather_cols(t, half0), carry)
            if t:
                carry = from_partner(m, t - 1, carry)
        activate(m, from_partner(m, PIECES - 1, carry))

    def phase_g(m):
        for t, off in enumerate(SUM_ORDER):
            piece = (z // 2 + off) % PIECES
            src = mo((1 - c) * HALF + piece * CH, CH)
            cols = pl.ds(mo(piece * CH, CH), CH)
            pc[m, :, cols] = jnp.dot(act_s[m], wd[:, pl.ds(src, CH)], preferred_element_type=F32).astype(BF)
            send(pc.at[m, :, cols], rsc.at[m, :, cols], s_d.at[m], rsc_r.at[m, t], partner)
        for off in SUM_ORDER:
            piece = (z // 2 + off) % PIECES
            src = mo(c * HALF + piece * CH, CH)
            cols = pl.ds(mo(piece * CH, CH), CH)
            part[m, :, cols] = jnp.dot(act_s[m], wd[:, pl.ds(src, CH)], preferred_element_type=F32)

    def phase_e(m):
        for t, off in enumerate(SUM_ORDER):
            cols = pl.ds(mo(((z // 2 + off) % 4) * CH, CH), CH)
            wait(rsc.at[m, :, cols], rsc_r.at[m, t])
            py[m, :, cols] = (part[m, :, cols] + rsc[m, :, cols].astype(F32)).astype(BF)
            for dy in (2, 1, 3):
                yy = (y + dy) % YS
                send(
                    py.at[m, pl.ds(mo(yy * RB, RB), RB), cols],
                    rsy.at[m, pl.ds((dy - 1) * RB, RB), cols],
                    s_e.at[m], rsy_r.at[m, t], at(s, yy, z, c),
                )

    def phase_f(m):
        last = s == SECTIONS - 1
        for t, off in enumerate(SUM_ORDER):
            piece = (z // 2 + off) % PIECES
            cols = pl.ds(mo(piece * CH, CH), CH)
            wait(rsy.at[m, :, cols], rsy_r.at[m, t])
            total = py[m, pl.ds(row0, RB), cols].astype(F32)
            for k in range(YS - 1):
                total = total + rsy[m, k * RB : (k + 1) * RB, cols].astype(F32)

            @pl.when(s < SECTIONS - 1)
            def _():
                pz[m, :, cols] = total.astype(BF)
                for e in range(2):
                    zz = piece * 2 + e
                    src = pz.at[m, :, pl.ds(mo(zz * FB, FB), FB)]
                    send(src, rsz.at[m, z], s_f.at[m], rsz_r.at[m], at(s + 1, y, zz, c))

            @pl.when(last)
            def _():
                for e in range(2):
                    pzf[m, :, piece * 2 + e, :] = total[:, e * FB : (e + 1) * FB]

        @pl.when(last)
        def _():
            pzf[m, :, z, :] = pzf[m, :, z, :] + xg[m, pl.ds(row0, RB), pl.ds(col0, FB)].astype(F32)

            def give(k, _):
                qq = ring(k)
                send(pzf.at[m, qq], orow_l.at[m, q], s_f.at[m], orl_r.at[m], (s, plane + qq))
                return 0

            lax.fori_loop(0, 15, give, 0)
            pltpu.make_async_copy(pzf.at[m, q], orow_l.at[m, q], orl_r.at[m]).start()

    phases = {"A": phase_a, "B": phase_b, "C": phase_c, "D": phase_d, "K": phase_k, "G": phase_g, "E": phase_e, "F": phase_f}

    def slot(n, _):
        for name, lag in SCHEDULE:
            m = n - lag

            if name in "DK":
                @pl.when(m == 0)
                def _():
                    for copy in weights:
                        copy.wait()

            @pl.when(jnp.logical_and(m >= 0, m < MB))
            def _():
                phases[name](m)

        return 0

    lax.fori_loop(0, SLOTS, slot, 0)

    @pl.when(s < SECTIONS - 1)
    def _():
        for m in range(MB):
            wait(oblk.at[m], ob_r.at[m])
            out_t[:, m, :] = oblk[m].astype(F32)

        def collect(k, _):
            qq = ring(k)
            send(out_t.at[qq], orow.at[b], or_s, or_r, (s, plane + qq))
            return 0

        lax.fori_loop(0, 15, collect, 0)
        orow[b] = out_t[q]
        wait(orow.at[pl.ds(0, 15)], or_r)

    @pl.when(s == SECTIONS - 1)
    def _():
        for m in range(MB):
            wait(orow_l.at[m], orl_r.at[m])
            for cc in range(2):
                total = orow_l[m, cc]
                for k in range(1, ZS):
                    total = total + orow_l[m, 2 * k + cc]
                orow[cc * ZS : (cc + 1) * ZS, m, :] = total

    for k in range(2 * ZS):
        out[:, k * FB : (k + 1) * FB] = orow[k, 0:MB, :].astype(BF)

    @pl.when(s == 0)
    def _():
        wait(tin_0.at[pl.ds(0, 15)], tin0_s)
        wait(tin.at[pl.ds(0, 15)], tin_s)

    @pl.when(s < SECTIONS - 1)
    def _():
        wait(orow.at[pl.ds(0, 15)], or_s)

    for m in range(MB):
        def gathered(m=m):
            wait(xg.at[m, pl.ds(0, RB), pl.ds(0, 7 * FB)], s_a.at[m])

        if m:
            gathered()
        else:
            pl.when(s > 0)(gathered)
        wait(xg.at[m, pl.ds(0, 3 * RB), pl.ds(0, HALF)], s_b.at[m])
        wait(xg.at[m, :, pl.ds(0, HALF)], s_c.at[m])
        wait(pc.at[m], s_d.at[m])
        wait(rsy.at[m], s_e.at[m])

        @pl.when(s < SECTIONS - 1)
        def _():
            wait(rsz.at[m], s_f.at[m])
            wait(res.at[m], s_res.at[m])

        @pl.when(s == SECTIONS - 1)
        def _():
            wait(orow_l.at[m, pl.ds(0, 15)], s_f.at[m])

        @pl.when(s > 0)
        def _():
            wait(oblk.at[m], s_ob.at[m])


def local(hidden_in, norm_gain, gate_weight, up_weight, down_weight, routes, route_weight):
    vmem = pl.BlockSpec(memory_space=pltpu.VMEM)
    hbm = pl.BlockSpec(memory_space=pl.ANY)
    dma = pltpu.SemaphoreType.DMA
    rows = pl.pallas_call(
        kernel,
        name="moe_layers",
        out_shape=jax.ShapeDtypeStruct((MB, D), BF),
        in_specs=[hbm] * 7,
        out_specs=vmem,
        scratch_shapes=[
            pltpu.VMEM((MB, D), BF),
            pltpu.VMEM((1, D), F32),
            pltpu.VMEM((1, MB, 8, ROWS), jnp.int32),
            pltpu.VMEM((1, MB, 8, ROWS), F32),
            pltpu.VMEM((D, FF), BF),
            pltpu.VMEM((D, FF), BF),
            pltpu.VMEM((FF, D), BF),
            pltpu.VMEM((MB, ROWS, D), BF),
            pltpu.VMEM((8, D), F32),
            pltpu.VMEM((16, 8, FB), F32),
            pltpu.VMEM((MB, ROWS, 128), F32),
            pltpu.VMEM((MB, ROWS, FF), BF),
            pltpu.VMEM((MB, ROWS, HALF), BF),
            pltpu.VMEM((MB, ROWS, HALF), BF),
            pltpu.VMEM((MB, ROWS, HALF), F32),
            pltpu.VMEM((MB, ROWS, HALF), BF),
            pltpu.VMEM((MB, 3 * RB, HALF), BF),
            pltpu.VMEM((MB, RB, HALF), BF),
            pltpu.VMEM((MB, ZS, RB, FB), BF),
            pltpu.VMEM((MB, RB, FB), BF),
            pltpu.VMEM((MB, RB, FB), BF),
            pltpu.VMEM((16, 8, FB), F32),
            pltpu.VMEM((16, 8, FB), F32),
            pltpu.VMEM((2, ZS, FB), F32),
            pltpu.VMEM((16, ZS, FB), F32),
            pltpu.VMEM((MB, 16, ZS, FB), F32),
            pltpu.VMEM((MB, 16, ZS, FB), F32),
            dma((7,)),
            dma, dma,
            dma, dma,
            dma((MB,)),
            dma((MB, ZS)),
            dma((MB, PIECES)),
            dma((MB, PIECES)),
            dma((MB, 4)),
            dma((MB, 4)),
            dma((MB,)),
            dma((MB,)),
            dma((MB,)),
            dma, dma,
            dma((MB,)), dma((MB,)), dma((MB,)), dma((MB,)), dma((MB,)), dma((MB,)), dma((MB,)), dma((MB,)),
        ],
        compiler_params=pltpu.CompilerParams(
            collective_id=0, has_side_effects=True, vmem_limit_bytes=60 << 20
        ),
        cost_estimate=pl.CostEstimate(
            flops=6 * MB * ROWS * D * FF, bytes_accessed=6 * D * FF, transcendentals=MB * ROWS * FF
        ),
    )(
        hidden_in.reshape(MB, D),
        norm_gain,
        gate_weight,
        up_weight,
        down_weight,
        jnp.swapaxes(routes, 2, 3),
        jnp.swapaxes(route_weight, 2, 3),
    )
    return rows[None, :, None, :]


def solution(mesh):
    return jax.shard_map(
        local,
        mesh=mesh,
        in_specs=(
            P(None, "ep", None),
            P("section", None),
            P("section", None, "ep"),
            P("section", None, "ep"),
            P("section", "ep", None),
            P("section", None, None, None),
            P("section", None, None, None),
        ),
        out_specs=P("section", None, "ep", None),
        check_vma=False,
    )
```

time: 157 us -> 133 us (0.85)
  Pallas kernels: 151 us -> 131 us
  local copies, waits for them, and re-layouts: 5.69 us -> 1.39 us
    pallas_call x1, Pallas kernels: 151 us -> 131 us  [local(): pl.pallas_call(kernel, name='moe_layers', out_shape=jax.ShapeDtypeStruct(...]
    unnamed x7 -> x1, local copies, waits for them, and re-layouts: 5.03 us -> 1.39 us
where the time goes in v2:
time: 133 us
  Pallas kernels  131 us (98%)
  local copies, waits for them, and re-layouts  1.39 us (1%)
    pallas_call x1, Pallas kernels, local(): pl.pallas_call(kernel, name='moe_layers', out_shape=jax.ShapeDtypeStruct(...  131 us

profile of v2, /device:TPU:7, one launch (start us, length us, event | category | flops | bytes accessed | tf_op | source)
XLA Modules:
  0.0 132.5 jit_solution(5199277663499185843)
XLA Ops:
  0.0 131.1 %moe_layers.1 = bf16[4,4096]{1,0:T(4,128)(2,1)} custom-call(bf16[4,4096]{1,0:T(4,128)(2,1)} %bitcast.5, f32[1,4096]{1,0:T(1,128)} %gain_hbm.1, bf16[1,4096,384]{2,1,0:T(8,128)(2,1)} %wg_hbm.1, bf16[1,4096,384]{2,1,0:T(8,128)(2,1)} %wu_hbm.1, bf16[1,384,4096]{2,1,0:T(8,128)(2,1)} %wd_hbm.1, s32[1,4,8,64]{3,2,1,0:T(8,128)} %bitcast.6, f32[1,4,8,64]{3,2,1,0:T(8,128)} %bitcast.7), custom_call_target="tpu_custom_call" | custom-call | flops 2415919104 | bytes 9437184 | tf_op jit(solution)/shard_map/moe_layers/pallas_call | solution.py:414
  131.2 1.4 %copy.9 = bf16[1,4,1,4096]{3,1,2,0:T(4,128)(2,1)} copy(bf16[1,4,1,4096]{3,1,2,0:T(4,128)(2,1)} %bitcast.4) | data formatting | bytes 65536

commit v3 on v2

--- a/solution.py
+++ b/solution.py
@@ -22,6 +22,7 @@
 HALF = D // 2
 CH = 512
 PIECES = HALF // CH
+GROUP = CH // FB
 FAR_FIRST = (4, 3, 5, 2, 6, 1, 7)
 GATHER_ORDER = (0, 1, 3, 2)
 SUM_ORDER = (2, 1, 3, 0)
@@ -112,7 +113,29 @@
     def _():
         lax.fori_loop(0, ZS, greet_last, 0)
 
-    for copy in small:
+    small[0].wait()
+    hin_f[...] = jnp.zeros_like(hin_f)
+    hin_f[0:MB, :] = hin[...].astype(F32)
+    for k in range(2 * ZS):
+        hin_0[k // ZS, k % ZS : k % ZS + 1, :] = hin_f[0:1, k * FB : (k + 1) * FB]
+
+    inner = jnp.logical_and(s > 0, s < SECTIONS - 1)
+    pl.semaphore_wait(barrier, jnp.where(inner, 18 + 2 * ZS, 18 + ZS))
+
+    def ring(k):
+        return (q + 8 + (1 - 2 * (k % 2)) * ((k + 1) // 2)) % 16
+
+    @pl.when(s == 0)
+    def _():
+        def spread_0(k, _):
+            qq = ring(k)
+            send(hin_0.at[qq % 2], tin_0.at[q], tin0_s, tin0_r, (s, plane + qq))
+            return 0
+
+        lax.fori_loop(0, 15, spread_0, 0)
+        pltpu.make_async_copy(hin_0.at[c], tin_0.at[q], tin0_r).start()
+
+    for copy in small[1:]:
         copy.wait()
     expert = ep // 4
     for m in range(MB):
@@ -120,27 +143,7 @@
         hit = jnp.sum(jnp.where(routes[0, m] == expert, rw, 0.0), axis=0, keepdims=True)
         share = hit / jnp.sum(rw, axis=0, keepdims=True)
         coeff[m] = jnp.swapaxes(jnp.broadcast_to(share, (128, ROWS)), 0, 1)
-    hin_f[...] = jnp.zeros_like(hin_f)
-    hin_f[0:MB, :] = hin[...].astype(F32)
-    for k in range(2 * ZS):
-        hin_0[k // ZS, k % ZS : k % ZS + 1, :] = hin_f[0:1, k * FB : (k + 1) * FB]
     out_t[...] = jnp.zeros_like(out_t)
-
-    inner = jnp.logical_and(s > 0, s < SECTIONS - 1)
-    pl.semaphore_wait(barrier, jnp.where(inner, 18 + 2 * ZS, 18 + ZS))
-
-    def ring(k):
-        return (q + 8 + (1 - 2 * (k % 2)) * ((k + 1) // 2)) % 16
-
-    @pl.when(s == 0)
-    def _():
-        def spread_0(k, _):
-            qq = ring(k)
-            send(hin_0.at[qq % 2], tin_0.at[q], tin0_s, tin0_r, (s, plane + qq))
-            return 0
-
-        lax.fori_loop(0, 15, spread_0, 0)
-        pltpu.make_async_copy(hin_0.at[c], tin_0.at[q], tin0_r).start()
 
     def block(m, yy, bb):
         return xg.at[m, pl.ds(mo(yy * RB, RB), RB), pl.ds(mo(bb * FB, FB), FB)]
@@ -163,37 +166,35 @@
             lax.fori_loop(0, 15, spread, 0)
             tin[q] = hin_f[:, pl.ds(col0, FB)]
 
-        @pl.when(jnp.logical_and(s == 0, m == 1))
-        def _():
-            wait(tin.at[pl.ds(0, 15)], tin_r)
+        mine = block(m, y, b)
+
+        def gather():
+            for off in FAR_FIRST:
+                send(mine, mine, s_a.at[m], agz_r.at[m, z], at(s, y, (z + off) % ZS, c))
 
         @pl.when(jnp.logical_and(s == 0, m > 0))
         def _():
+            @pl.when(m == 1)
+            def _():
+                wait(tin.at[pl.ds(0, 15)], tin_r)
+
             xg[m, pl.ds(row0, RB), pl.ds(col0, FB)] = tin[:, m, :].astype(BF)
+            gather()
 
         @pl.when(s > 0)
         def _():
             wait(res.at[m], res_r.at[m])
+            total = res[m].astype(F32)
             wait(rsz.at[m], rsz_r.at[m])
-            total = res[m].astype(F32)
             for k in range(ZS):
                 total = total + rsz[m, k].astype(F32)
             xg[m, pl.ds(row0, RB), pl.ds(col0, FB)] = total.astype(BF)
-
-        mine = block(m, y, b)
-
-        @pl.when(jnp.logical_not(first))
-        def _():
-            for off in FAR_FIRST:
-                send(mine, mine, s_a.at[m], agz_r.at[m, z], at(s, y, (z + off) % ZS, c))
+            gather()
+            send(mine, oblk.at[m], s_ob.at[m], ob_r.at[m], at(s - 1, y, z, c))
 
         @pl.when(s < SECTIONS - 1)
         def _():
             send(mine, res.at[m], s_res.at[m], res_r.at[m], at(s + 1, y, z, c))
-
-        @pl.when(s > 0)
-        def _():
-            send(mine, oblk.at[m], s_ob.at[m], ob_r.at[m], at(s - 1, y, z, c))
 
     def gather_cols(t, start):
         return pl.ds(mo(start + ((z // 2 + GATHER_ORDER[t]) % PIECES) * CH, CH), CH)
@@ -252,15 +253,6 @@
         for t in range(PIECES):
             carry = from_partner(m, t, carry)
         activate(m, carry)
-
-    def phase_k(m):
-        carry = start_sums()
-        for t in range(PIECES):
-            to_partner(m, t)
-            carry = products(m, gather_cols(t, half0), carry)
-            if t:
-                carry = from_partner(m, t - 1, carry)
-        activate(m, from_partner(m, PIECES - 1, carry))
 
     def phase_g(m):
         for t, off in enumerate(SUM_ORDER):
@@ -289,30 +281,32 @@
                 )
 
     def phase_f(m):
-        last = s == SECTIONS - 1
-        for t, off in enumerate(SUM_ORDER):
-            piece = (z // 2 + off) % PIECES
+        def total_of(t):
+            piece = (z // GROUP + SUM_ORDER[t]) % PIECES
             cols = pl.ds(mo(piece * CH, CH), CH)
             wait(rsy.at[m, :, cols], rsy_r.at[m, t])
             total = py[m, pl.ds(row0, RB), cols].astype(F32)
             for k in range(YS - 1):
                 total = total + rsy[m, k * RB : (k + 1) * RB, cols].astype(F32)
-
-            @pl.when(s < SECTIONS - 1)
-            def _():
+            return piece, cols, total
+
+        @pl.when(s < SECTIONS - 1)
+        def _():
+            for t in range(PIECES):
+                piece, cols, total = total_of(t)
                 pz[m, :, cols] = total.astype(BF)
-                for e in range(2):
-                    zz = piece * 2 + e
+                for e in range(GROUP):
+                    zz = piece * GROUP + e
                     src = pz.at[m, :, pl.ds(mo(zz * FB, FB), FB)]
                     send(src, rsz.at[m, z], s_f.at[m], rsz_r.at[m], at(s + 1, y, zz, c))
 
-            @pl.when(last)
-            def _():
-                for e in range(2):
-                    pzf[m, :, piece * 2 + e, :] = total[:, e * FB : (e + 1) * FB]
-
-        @pl.when(last)
-        def _():
+        @pl.when(s == SECTIONS - 1)
+        def _():
+            for t in range(PIECES):
+                piece, cols, total = total_of(t)
+                for e in range(GROUP):
+                    pzf[m, :, piece * GROUP + e, :] = total[:, e * FB : (e + 1) * FB]
+
             pzf[m, :, z, :] = pzf[m, :, z, :] + xg[m, pl.ds(row0, RB), pl.ds(col0, FB)].astype(F32)
 
             def give(k, _):
@@ -323,13 +317,13 @@
             lax.fori_loop(0, 15, give, 0)
             pltpu.make_async_copy(pzf.at[m, q], orow_l.at[m, q], orl_r.at[m]).start()
 
-    phases = {"A": phase_a, "B": phase_b, "C": phase_c, "D": phase_d, "K": phase_k, "G": phase_g, "E": phase_e, "F": phase_f}
+    phases = {"A": phase_a, "B": phase_b, "C": phase_c, "D": phase_d, "G": phase_g, "E": phase_e, "F": phase_f}
 
     def slot(n, _):
         for name, lag in SCHEDULE:
             m = n - lag
 
-            if name in "DK":
+            if name == "D":
                 @pl.when(m == 0)
                 def _():
                     for copy in weights:

time: 133 us -> 133 us (level)
  no operation moved by 1% of the time
where the time goes in v3:
time: 133 us
  Pallas kernels  131 us (98%)
  local copies, waits for them, and re-layouts  1.39 us (1%)
    pallas_call x1, Pallas kernels, local(): pl.pallas_call(kernel, name='moe_layers', out_shape=jax.ShapeDtypeStruct(...  131 us

profile of v3, /device:TPU:7, one launch (start us, length us, event | category | flops | bytes accessed | tf_op | source)
XLA Modules:
  0.0 132.7 jit_solution(13203134907365571106)
XLA Ops:
  0.0 131.3 %moe_layers.1 = bf16[4,4096]{1,0:T(4,128)(2,1)} custom-call(bf16[4,4096]{1,0:T(4,128)(2,1)} %bitcast.5, f32[1,4096]{1,0:T(1,128)} %gain_hbm.1, bf16[1,4096,384]{2,1,0:T(8,128)(2,1)} %wg_hbm.1, bf16[1,4096,384]{2,1,0:T(8,128)(2,1)} %wu_hbm.1, bf16[1,384,4096]{2,1,0:T(8,128)(2,1)} %wd_hbm.1, s32[1,4,8,64]{3,2,1,0:T(8,128)} %bitcast.6, f32[1,4,8,64]{3,2,1,0:T(8,128)} %bitcast.7), custom_call_target="tpu_custom_call" | custom-call | flops 2415919104 | bytes 9437184 | tf_op jit(solution)/shard_map/moe_layers/pallas_call | solution.py:408
  131.3 1.4 %copy.9 = bf16[1,4,1,4096]{3,1,2,0:T(4,128)(2,1)} copy(bf16[1,4,1,4096]{3,1,2,0:T(4,128)(2,1)} %bitcast.4) | data formatting | bytes 65536

commit v4 on v3

--- a/solution.py
+++ b/solution.py
@@ -149,7 +149,7 @@
         return xg.at[m, pl.ds(mo(yy * RB, RB), RB), pl.ds(mo(bb * FB, FB), FB)]
 
     def phase_a(m):
-        first = jnp.logical_and(s == 0, m == 0)
+        first = jnp.logical_and(s == 0, jnp.bool_(m == 0))
 
         @pl.when(first)
         def _():
@@ -172,9 +172,9 @@
             for off in FAR_FIRST:
                 send(mine, mine, s_a.at[m], agz_r.at[m, z], at(s, y, (z + off) % ZS, c))
 
-        @pl.when(jnp.logical_and(s == 0, m > 0))
-        def _():
-            @pl.when(m == 1)
+        @pl.when(jnp.logical_and(s == 0, jnp.bool_(m > 0)))
+        def _():
+            @pl.when(jnp.bool_(m == 1))
             def _():
                 wait(tin.at[pl.ds(0, 15)], tin_r)
 
@@ -201,7 +201,7 @@
 
     def phase_b(m):
         for t in range(PIECES):
-            @pl.when(jnp.logical_or(s > 0, m > 0))
+            @pl.when(jnp.logical_or(s > 0, jnp.bool_(m > 0)))
             def _():
                 pair = ((z // 2 + GATHER_ORDER[t]) % PIECES) * 2
                 for zz in (pair + 1 - z % 2,) if t == 0 else (pair, pair + 1):
@@ -319,23 +319,12 @@
 
     phases = {"A": phase_a, "B": phase_b, "C": phase_c, "D": phase_d, "G": phase_g, "E": phase_e, "F": phase_f}
 
-    def slot(n, _):
-        for name, lag in SCHEDULE:
-            m = n - lag
-
-            if name == "D":
-                @pl.when(m == 0)
-                def _():
-                    for copy in weights:
-                        copy.wait()
-
-            @pl.when(jnp.logical_and(m >= 0, m < MB))
-            def _():
-                phases[name](m)
-
-        return 0
-
-    lax.fori_loop(0, SLOTS, slot, 0)
+    steps = [(name, n - lag) for n in range(SLOTS) for name, lag in SCHEDULE if 0 <= n - lag < MB]
+    for name, m in steps:
+        if (name, m) == ("D", 0):
+            for copy in weights:
+                copy.wait()
+        phases[name](m)
 
     @pl.when(s < SECTIONS - 1)
     def _():

time: 133 us -> 133 us (level)
  no operation moved by 1% of the time
where the time goes in v4:
time: 133 us
  Pallas kernels  131 us (98%)
  local copies, waits for them, and re-layouts  1.39 us (1%)
    pallas_call x1, Pallas kernels, local(): pl.pallas_call(kernel, name='moe_layers', out_shape=jax.ShapeDtypeStruct(...  131 us

profile of v4, /device:TPU:7, one launch (start us, length us, event | category | flops | bytes accessed | tf_op | source)
XLA Modules:
  0.0 132.7 jit_solution(17252994670445411195)
XLA Ops:
  0.0 131.3 %moe_layers.1 = bf16[4,4096]{1,0:T(4,128)(2,1)} custom-call(bf16[4,4096]{1,0:T(4,128)(2,1)} %bitcast.5, f32[1,4096]{1,0:T(1,128)} %gain_hbm.1, bf16[1,4096,384]{2,1,0:T(8,128)(2,1)} %wg_hbm.1, bf16[1,4096,384]{2,1,0:T(8,128)(2,1)} %wu_hbm.1, bf16[1,384,4096]{2,1,0:T(8,128)(2,1)} %wd_hbm.1, s32[1,4,8,64]{3,2,1,0:T(8,128)} %bitcast.6, f32[1,4,8,64]{3,2,1,0:T(8,128)} %bitcast.7), custom_call_target="tpu_custom_call" | custom-call | flops 2415919104 | bytes 9437184 | tf_op jit(solution)/shard_map/moe_layers/pallas_call | solution.py:397
  131.3 1.4 %copy.9 = bf16[1,4,1,4096]{3,1,2,0:T(4,128)(2,1)} copy(bf16[1,4,1,4096]{3,1,2,0:T(4,128)(2,1)} %bitcast.4) | data formatting | bytes 65536
